TPU v7x, 32 devices: a whole 2x2x4 slice. The times are simulated.
32 devices in a mesh: seq: 4 (over z), col: 4 (over x, core), batch: 2 (over y).
Axes of the slice: x: 2, y: 2, z: 4, core: 2. Of those that a mesh axis runs over, the one named last changes fastest.
Arguments:
- tokens: int32 [2, 262144], P('batch', ('seq', 'col')), may hold values from 0 to 3
- stem_weight: bfloat16 [64, 768], replicated, may hold values from -1.5 to 1.5
- conv_weight: bfloat16 [3840, 768], replicated, may hold values from -0.09375 to 0.09375
- conv_bias: float32 [768], replicated, may hold values from -1 to 1
- up_weight: bfloat16 [768, 1536], replicated, may hold values from -0.21875 to 0.21875
- norm_gain: float32 [1536], replicated, may hold values from 0.1 to 1.9
- pair_weight: bfloat16 [1536, 64], replicated, may hold values from -0.15625 to 0.15625
- out_weight: bfloat16 [1024, 128], replicated, may hold values from -0.1875 to 0.1875
- cotangent: bfloat16 [2, 128, 128, 128], P('batch', 'seq', 'col'), may hold values from -24 to 24
- projection: float32 [768, 128], replicated, may hold values from -0.21875 to 0.21875
- buckets: int32 [3840], replicated, may hold values from 0 to 31
Outputs:
- input_grad: bfloat16 [2, 16384, 768], P('batch', ('seq', 'col'))
- embedding: float32 [2, 32, 128], P('batch')
All inputs are finite; a program needn't handle non-finite values.
Results may differ from a plain program's by a relative error of at most 0.012.
Values may be sent and summed in bfloat16 or wider, within the bound.
A program may use at most 128 MiB of HBM per device.

v0:
```python
import jax
import jax.numpy as jnp
from jax import lax
from jax.sharding import PartitionSpec as P

OP = 32
PATCH = 16
POOL = 128
BUCKETS = 32


highest = lax.Precision.HIGHEST


def extended(cells, sides, width):
    for axis, dim in sides:
        count = lax.axis_size(axis)
        ends = count - 1
        head = lax.slice_in_dim(cells, 0, width, axis=dim)
        tail = lax.slice_in_dim(cells, cells.shape[dim] - width, cells.shape[dim], axis=dim)
        cells = jnp.concatenate(
            [
                lax.ppermute(tail, axis, [(i, (i + 1) % count) for i in range(ends)]),
                cells,
                lax.ppermute(head, axis, [((i + 1) % count, i) for i in range(ends)]),
            ],
            axis=dim,
        )
    return cells


def split_pair(values):
    upper = values.astype(jnp.bfloat16)
    lower = (values - upper.astype(jnp.float32)).astype(jnp.bfloat16)
    return (upper, lower)


def shards(
    tokens,
    stem_weight,
    conv_weight,
    conv_bias,
    up_weight,
    norm_gain,
    pair_weight,
    out_weight,
    cotangent,
    projection,
    buckets,
):
    channels = conv_weight.shape[1]
    kernel = conv_weight.shape[0] // channels
    reach = (kernel - 1) // 2
    patches = tokens.shape[1] // PATCH
    bins_dev = patches // POOL
    bases = tokens[0].reshape(patches, PATCH)
    onehot = (
        (bases[:, :, None] == jnp.arange(4, dtype=jnp.int32))
        .astype(jnp.bfloat16)
        .reshape(patches, PATCH * 4)
    )
    embedded = jnp.dot(onehot, stem_weight, preferred_element_type=jnp.float32).astype(jnp.bfloat16)
    padded = extended(embedded, ((("seq", "col"), 0),), reach)
    unfolded = jnp.concatenate(
        [padded[offset : offset + patches] for offset in range(kernel)], axis=1
    )
    before = jnp.dot(unfolded, conv_weight, preferred_element_type=jnp.float32) + conv_bias
    after, gelu_back = jax.vjp(jax.nn.gelu, before)
    pooled = jnp.mean(after.reshape(bins_dev, POOL, channels), axis=1).astype(jnp.bfloat16)
    hidden = jnp.dot(pooled, up_weight, preferred_element_type=jnp.float32)
    inverse = lax.rsqrt(jnp.mean(hidden * hidden, axis=1, keepdims=True) + 1e-06)
    normed = (hidden * inverse * norm_gain).astype(jnp.bfloat16)
    seq_count = lax.axis_size("seq")
    col_count = lax.axis_size("col")
    row_len = bins_dev * col_count
    col_len = bins_dev * seq_count
    all_bins = row_len * seq_count
    row_index = lax.axis_index("seq")
    col_index = lax.axis_index("col")
    every = lax.all_gather(normed, ("seq", "col"), axis=0, tiled=True)
    row_part = lax.dynamic_slice_in_dim(every, row_index * row_len, row_len, 0)
    col_part = lax.dynamic_slice_in_dim(every, col_index * col_len, col_len, 0)
    left = jnp.dot(row_part, pair_weight[:, :OP], preferred_element_type=jnp.float32).astype(
        jnp.bfloat16
    )
    right = jnp.dot(col_part, pair_weight[:, OP:], preferred_element_type=jnp.float32).astype(
        jnp.bfloat16
    )
    pair_channels = cotangent.shape[3]
    blocks = cotangent[0].reshape(col_count, bins_dev, col_len, pair_channels)
    left_groups = left.astype(jnp.float32).reshape(col_count, bins_dev, OP)
    right_wide = right.astype(jnp.float32)

    def pair_step(carry, inputs):
        block, rows_left = inputs
        outer_grad = lax.dot_general(
            block.reshape(bins_dev * col_len, pair_channels),
            out_weight,
            (((1,), (1,)), ((), ())),
            preferred_element_type=jnp.float32,
        ).reshape(bins_dev, col_len, OP, OP)
        grad_left = jnp.einsum("ijkl,jl->ik", outer_grad, right_wide, precision=highest)
        carry = carry + jnp.einsum("ijkl,ik->jl", outer_grad, rows_left, precision=highest)
        return (carry, grad_left)

    grad_right, grad_left = lax.scan(
        pair_step, jnp.zeros((col_len, OP), jnp.float32), (blocks, left_groups)
    )
    grad_left = grad_left.reshape(row_len, OP)
    row_term = lax.dot_general(
        grad_left,
        pair_weight[:, :OP].astype(jnp.float32),
        (((1,), (1,)), ((), ())),
        precision=highest,
    )
    col_term = lax.dot_general(
        grad_right,
        pair_weight[:, OP:].astype(jnp.float32),
        (((1,), (1,)), ((), ())),
        precision=highest,
    )
    empty_rows = jnp.zeros((all_bins, row_term.shape[1]), jnp.float32)
    placed = lax.dynamic_update_slice_in_dim(
        empty_rows, row_term, row_index * row_len, 0
    ) + lax.dynamic_update_slice_in_dim(empty_rows, col_term, col_index * col_len, 0)
    d_normed = lax.psum_scatter(placed, ("seq", "col"), scatter_dimension=0, tiled=True)
    scaled = d_normed * norm_gain
    inner = jnp.mean(scaled * hidden, axis=1, keepdims=True)
    d_hidden = inverse * scaled - hidden * inverse**3 * inner
    d_pooled = lax.dot_general(
        d_hidden, up_weight.astype(jnp.float32), (((1,), (1,)), ((), ())), precision=highest
    )
    spread = jnp.broadcast_to(d_pooled[:, None, :] / POOL, (bins_dev, POOL, channels)).reshape(
        patches, channels
    )
    d_before = gelu_back(spread)[0].astype(jnp.bfloat16)
    grads_padded = extended(d_before, ((("seq", "col"), 0),), reach)
    stacked = jnp.stack(
        [
            grads_padded[2 * reach - offset : 2 * reach - offset + patches]
            for offset in range(kernel)
        ],
        axis=1,
    )
    input_grad = jnp.einsum(
        "tko,kio->ti",
        stacked,
        conv_weight.reshape(kernel, channels, channels),
        preferred_element_type=jnp.float32,
    ).astype(jnp.bfloat16)
    proj_upper, proj_lower = split_pair(projection)
    through = jnp.dot(d_before, proj_upper, preferred_element_type=jnp.float32) + jnp.dot(
        d_before, proj_lower, preferred_element_type=jnp.float32
    )
    through_upper, through_lower = split_pair(through)
    contract = (((0,), (0,)), ((), ()))
    projected = lax.dot_general(
        unfolded, through_upper, contract, preferred_element_type=jnp.float32
    ) + lax.dot_general(unfolded, through_lower, contract, preferred_element_type=jnp.float32)
    member = (buckets[None, :] == jnp.arange(BUCKETS, dtype=jnp.int32)[:, None]).astype(jnp.float32)
    sketch = lax.psum(jnp.dot(member, projected, precision=highest), ("seq", "col"))
    unit = sketch * lax.rsqrt(jnp.mean(sketch * sketch) + 1e-06)
    center = lax.psum(unit, "batch") / lax.axis_size("batch")
    return (input_grad[None], (unit - center)[None])


def solution(mesh):
    in_specs = (
        P("batch", ("seq", "col")),
        P(),
        P(),
        P(),
        P(),
        P(),
        P(),
        P(),
        P("batch", "seq", "col", None),
        P(),
        P(),
    )
    out_specs = (P("batch", ("seq", "col"), None), P("batch", None, None))
    return jax.shard_map(shards, mesh=mesh, in_specs=in_specs, out_specs=out_specs, check_vma=False)
```

profile of v0, /device:TPU:0, one launch (start us, length us, event | category | flops | bytes accessed | tf_op | source)
XLA Modules:
  0.0 287.7 jit_solution(4605901416483217111)
XLA Ops:
  7.7 1.8 reduce.3
  10.2 1.6 convolution_convert_fusion
  12.9 2.4 collective-permute-start
  15.3 1.3 collective-permute-start.1
  16.6 1.9 fusion.28
  19.1 1.3 collective-permute-done.1
  21.3 8.4 %bitcast_reduce_fusion = (f32[8,768]{1,0:T(8,128)S(1)}, f32[1024,768]{1,0:T(8,128)}) fusion(f32[768]{0:T(1024)S(1)} %copy-done.12, bf16[1024,3840]{1,0:T(8,128)(2,1)S(1)} %fusion.33, bf16[3840,768]{1,0:T(8,128)(2,1)S(1)} %bitcast.121), kind=kOutput, calls=%fused_computation.27 | convolution fusion | flops 6047655936 | bytes 16935936 | tf_op jit(solution)/shard_map/dot_general | solution.py:67
  30.4 25.4 %all_gather.3 = bf16[128,1536]{1,0:T(8,128)(2,1)S(1)} all-gather(bf16[8,1536]{1,0:T(8,128)(2,1)S(1)} %multiply_convert_fusion), channel_id=1, replica_groups=mesh['seq'=4,'col'=4,'batch'=2] {'seq','col'}, dimensions={0}, use_global_device_ids=true | all-gather | bytes 417792 | tf_op jit(solution)/shard_map/all_gather | solution.py:80
  56.0 67.3 %while.13 = (s32[]{:T(128)}, f32[32,32]{1,0:T(8,128)S(1)}, f32[4,8,32]{2,1,0:T(8,128)S(1)}, bf16[4,8,32,128]{3,2,1,0:T(8,128)(2,1)}, bf16[1024,128]{1,0:T(8,128)...) while((s32[]{:T(128)}, f32[32,32]{1,0:T(8,128)S(1)}, ...), condition=%wide.region_3.4_spmd.clone, body=%wide.region_2.3_spmd.clone.sunk | while | flops 73402368 | bytes 3512939 | solution.py:106
  56.2 1.6 fusion.103
  57.7 10.4 %fusion.104 = f32[1,8,32,1]{2,0,3,1:T(1,128)S(1)} fusion(f32[32,32,1,1]{1,2,0,3:T(1,128)S(1)} %bitcast.116, f32[8,32,32,32]{3,1,2,0:T(8,128)S(1)} %fusion.103), kind=kOutput, calls=%fused_computation.clone.1 | convolution fusion | flops 3145728 | bytes 1053696 | tf_op jit(solution)/shard_map/while/body/eval_jaxpr/ijkl,jl->ik/dot_general | solution.py:102
  68.2 4.7 %fusion.105 = f32[1,32,32,1]{2,0,3,1:T(1,128)S(1)} fusion(f32[8,32,1,1]{1,2,0,3:T(1,128)S(1)} %bitcast.118, f32[8,32,32,32]{3,1,2,0:T(8,128)S(1)} %fusion.103), kind=kOutput, calls=%fused_computation.2.clone.1 | convolution fusion | flops 3145728 | bytes 1053696 | tf_op jit(solution)/shard_map/while/body/eval_jaxpr/ijkl,ik->jl/dot_general | solution.py:103
  72.9 1.6 fusion.103
  74.5 10.4 %fusion.104 = f32[1,8,32,1]{2,0,3,1:T(1,128)S(1)} fusion(f32[32,32,1,1]{1,2,0,3:T(1,128)S(1)} %bitcast.116, f32[8,32,32,32]{3,1,2,0:T(8,128)S(1)} %fusion.103), kind=kOutput, calls=%fused_computation.clone.1 | convolution fusion | flops 3145728 | bytes 1053696 | tf_op jit(solution)/shard_map/while/body/eval_jaxpr/ijkl,jl->ik/dot_general | solution.py:102
  84.9 4.7 %fusion.105 = f32[1,32,32,1]{2,0,3,1:T(1,128)S(1)} fusion(f32[8,32,1,1]{1,2,0,3:T(1,128)S(1)} %bitcast.118, f32[8,32,32,32]{3,1,2,0:T(8,128)S(1)} %fusion.103), kind=kOutput, calls=%fused_computation.2.clone.1 | convolution fusion | flops 3145728 | bytes 1053696 | tf_op jit(solution)/shard_map/while/body/eval_jaxpr/ijkl,ik->jl/dot_general | solution.py:103
  89.7 1.6 fusion.103
  91.2 10.4 %fusion.104 = f32[1,8,32,1]{2,0,3,1:T(1,128)S(1)} fusion(f32[32,32,1,1]{1,2,0,3:T(1,128)S(1)} %bitcast.116, f32[8,32,32,32]{3,1,2,0:T(8,128)S(1)} %fusion.103), kind=kOutput, calls=%fused_computation.clone.1 | convolution fusion | flops 3145728 | bytes 1053696 | tf_op jit(solution)/shard_map/while/body/eval_jaxpr/ijkl,jl->ik/dot_general | solution.py:102
  101.7 4.7 %fusion.105 = f32[1,32,32,1]{2,0,3,1:T(1,128)S(1)} fusion(f32[8,32,1,1]{1,2,0,3:T(1,128)S(1)} %bitcast.118, f32[8,32,32,32]{3,1,2,0:T(8,128)S(1)} %fusion.103), kind=kOutput, calls=%fused_computation.2.clone.1 | convolution fusion | flops 3145728 | bytes 1053696 | tf_op jit(solution)/shard_map/while/body/eval_jaxpr/ijkl,ik->jl/dot_general | solution.py:103
  106.4 1.6 fusion.103
  108.0 10.4 %fusion.104 = f32[1,8,32,1]{2,0,3,1:T(1,128)S(1)} fusion(f32[32,32,1,1]{1,2,0,3:T(1,128)S(1)} %bitcast.116, f32[8,32,32,32]{3,1,2,0:T(8,128)S(1)} %fusion.103), kind=kOutput, calls=%fused_computation.clone.1 | convolution fusion | flops 3145728 | bytes 1053696 | tf_op jit(solution)/shard_map/while/body/eval_jaxpr/ijkl,jl->ik/dot_general | solution.py:102
  118.4 4.7 %fusion.105 = f32[1,32,32,1]{2,0,3,1:T(1,128)S(1)} fusion(f32[8,32,1,1]{1,2,0,3:T(1,128)S(1)} %bitcast.118, f32[8,32,32,32]{3,1,2,0:T(8,128)S(1)} %fusion.103), kind=kOutput, calls=%fused_computation.2.clone.1 | convolution fusion | flops 3145728 | bytes 1053696 | tf_op jit(solution)/shard_map/while/body/eval_jaxpr/ijkl,ik->jl/dot_general | solution.py:103
  124.8 54.0 %reduce-scatter.2.cloned.1.call-done = f32[8,1536]{1,0:T(8,128)} async-done(((f32[128,1536]{1,0:T(8,128)}), f32[8,1536]{1,0:T(8,128)}) %reduce-scatter.2.cloned.1.call-update) | async-done | bytes 49168 | tf_op jit(solution)/shard_map/reduce_scatter | solution.py:126
  179.7 2.8 convolution_multiply_fusion
  182.5 3.7 %fusion.14 = bf16[1024,768]{1,0:T(8,128)(2,1)S(1)} fusion(f32[1024,768]{1,0:T(8,128)} %get-tuple-element.89, f32[8,768]{1,0:T(8,128)S(1)} %convolution_multiply_fusion, f32[768]{0:T(1024)S(1)} %copy-done.12), kind=kLoop, calls=%fused_computation.22 | loop fusion | flops 16515072 | bytes 4746240 | tf_op jit(solution)/shard_map/convert_element_type | solution.py:136
  187.9 5.8 %fusion.40 = f32[3840,128]{1,0:T(8,128)S(1)} fusion(bf16[1024,3840]{1,0:T(8,128)(2,1)} %copy-done.3, f32[1024,128]{1,0:T(8,128)S(1)} %convolution_add_fusion.2), kind=kOutput, calls=%fused_computation.74 | convolution fusion | flops 1007157248 | bytes 10354688 | tf_op jit(solution)/shard_map/dot_general | solution.py:159
  193.8 2.3 convolution_add_fusion
  196.8 57.6 %psum.14 = f32[32,128]{1,0:T(8,128)S(1)} all-reduce(f32[32,128]{1,0:T(8,128)S(1)} %fusion.39), channel_id=1, replica_groups=mesh['seq'=4,'col'=4,'batch'=2] {'seq','col'}, use_global_device_ids=true, to_apply=%region_6.7 | all-reduce | flops 4096 | bytes 32768 | tf_op jit(solution)/shard_map/psum | solution.py:161
  255.8 8.2 %psum.15 = f32[32,128]{1,0:T(8,128)S(1)} all-reduce(f32[32,128]{1,0:T(8,128)S(1)} %broadcast_multiply_fusion), channel_id=1, replica_groups=mesh['seq'=4,'col'=4,'batch'=2] {'batch'}, use_global_device_ids=true, to_apply=%region_8.9 | all-reduce | flops 4096 | bytes 32768 | tf_op jit(solution)/shard_map/psum | solution.py:163
  263.9 1.4 collective-permute-start.2
  266.0 3.0 %collective-permute-start.3 = (bf16[2,768]{1,0:T(2,128)(2,1)S(1)}, bf16[2,768]{1,0:T(2,128)(2,1)S(1)}, u32[]{:S(2)}, u32[]{:S(2)}) collective-permute-start(bf16[2,768]{1,0:T(2,128)(2,1)S(1)} %get-tuple-element.82), channel_id=1, source_target_pairs={{0,2},{2,4},{4,6},{6,8},{8,10},{10,12},{12,14},{14,16},{16,18},{18... | collective-permute-start | bytes 9224 | tf_op jit(solution)/shard_map/ppermute | solution.py:23
  269.0 1.9 fusion.24
  273.5 7.4 %fusion.35 = bf16[1,1024,768]{2,1,0:T(8,128)(2,1)} fusion(bf16[1024,5,768]{2,0,1:T(8,128)(2,1)S(1)} %fusion.30, bf16[5,768,768]{2,1,0:T(8,128)(2,1)S(1)} %bitcast.124), kind=kOutput, calls=%fused_computation.62 | convolution fusion | flops 6040584192 | bytes 15335424 | tf_op jit(solution)/shard_map/tko,kio->ti/dot_general | solution.py:145
  (89 shorter events, 13.2 us)
Async XLA Ops:
  7.2 22.6 %copy-start = (bf16[768,1536]{1,0:T(8,128)(2,1)S(1)}, bf16[768,1536]{1,0:T(8,128)(2,1)}, u32[]{:S(2)}) copy-start(bf16[768,1536]{1,0:T(8,128)(2,1)} %param.17) | copy-start | bytes 7077892
  7.2 171.6 %reduce-scatter.2.cloned.1.call-start = ((), (), s32[]{:S(2)}) async-start(), calls=%async_computation.1 | async-start | bytes 835584 | tf_op jit(solution)/shard_map/reduce_scatter | solution.py:126
  11.7 1.1 copy-start.4
  12.9 3.7 %collective-permute-start = (bf16[2,768]{1,0:T(2,128)(2,1)S(1)}, bf16[2,768]{1,0:T(2,128)(2,1)S(1)}, u32[]{:S(2)}, u32[]{:S(2)}) collective-permute-start(bf16[2,768]{1,0:T(2,128)(2,1)S(1)} %get-tuple-element.85), channel_id=1, source_target_pairs={{0,2},{2,4},{4,6},{6,8},{8,10},{10,12},{12,14},{14,16},{16,18},{18... | collective-permute-start | bytes 9224 | tf_op jit(solution)/shard_map/ppermute | solution.py:23
  15.3 5.2 %collective-permute-start.1 = (bf16[2,768]{1,0:T(2,128)(2,1)S(1)}, bf16[2,768]{1,0:T(2,128)(2,1)S(1)}, u32[]{:S(2)}, u32[]{:S(2)}) collective-permute-start(bf16[2,768]{1,0:T(2,128)(2,1)S(1)} %get-tuple-element.84), channel_id=1, source_target_pairs={{2,0},{4,2},{6,4},{8,6},{10,8},{12,10},{14,12},{16,14},{18,16},{20... | collective-permute-start | bytes 9224 | tf_op jit(solution)/shard_map/ppermute | solution.py:25
  16.6 2.0 copy-start.5
  16.6 4.6 %slice-start.2 = ((s8[5898240]{0:T(1024)(128)(4,1)}), s8[4194304]{0:T(1024)(128)(4,1)S(1)}, s32[]{:S(2)}) async-start(s8[5898240]{0:T(1024)(128)(4,1)} %bitcast.120), calls=%async_computation.4 | async-start | bytes 8388608
  19.0 2.3 slice-start.3
  19.1 2.1 copy-start.12
  21.2 8.5 %copy-start.3 = (bf16[1024,3840]{1,0:T(8,128)(2,1)}, bf16[1024,3840]{1,0:T(8,128)(2,1)S(1)}, u32[]{:S(2)}) copy-start(bf16[1024,3840]{1,0:T(8,128)(2,1)S(1)} %fusion.33) | copy-start | bytes 23592964
  21.3 9.0 %copy-start.10 = (f32[1536]{0:T(1024)S(1)}, f32[1536]{0:T(1024)}, u32[]{:S(2)}) copy-start(f32[1536]{0:T(1024)} %param.18) | copy-start | bytes 18436
  21.3 34.5 %copy-start.9 = (bf16[1536,64]{0,1:T(8,128)(2,1)S(1)}, bf16[1536,64]{0,1:T(8,128)(2,1)}, u32[]{:S(2)}) copy-start(bf16[1536,64]{0,1:T(8,128)(2,1)} %param.19) | copy-start | bytes 589828
  29.7 26.3 %copy-start.6 = (bf16[1024,128]{1,0:T(8,128)(2,1)S(1)}, bf16[1024,128]{1,0:T(8,128)(2,1)}, u32[]{:S(2)}) copy-start(bf16[1024,128]{1,0:T(8,128)(2,1)} %param.20) | copy-start | bytes 786436
  123.9 0.9 copy-start.7
  179.7 6.5 %copy-start.8 = (f32[768,128]{1,0:T(8,128)S(1)}, f32[768,128]{1,0:T(8,128)}, u32[]{:S(2)}) copy-start(f32[768,128]{1,0:T(8,128)} %param.22) | copy-start | bytes 1179652
  186.2 1.1 copy-start.1
  187.3 6.4 %slice-start = ((s8[7864320]{0:T(1024)(128)(4,1)}), s8[4194304]{0:T(1024)(128)(4,1)S(1)}, s32[]{:S(2)}) async-start(s8[7864320]{0:T(1024)(128)(4,1)} %bitcast.112), calls=%async_computation.2 | async-start | bytes 8388608
  187.9 5.8 %slice-start.1 = ((s8[7864320]{0:T(1024)(128)(4,1)}), s8[3670016]{0:T(1024)(128)(4,1)S(1)}, s32[]{:S(2)}) async-start(s8[7864320]{0:T(1024)(128)(4,1)} %bitcast.112), calls=%async_computation.3 | async-start | bytes 7340032
  193.7 2.3 copy-start.11
  263.9 7.0 %copy-start.2 = (bf16[1024,768]{1,0:T(8,128)(2,1)S(1)}, bf16[1024,768]{1,0:T(8,128)(2,1)}, u32[]{:S(2)}) copy-start(bf16[1024,768]{1,0:T(8,128)(2,1)} %copy-done.1) | copy-start | bytes 4718596
  263.9 5.1 %collective-permute-start.2 = (bf16[2,768]{1,0:T(2,128)(2,1)S(1)}, bf16[2,768]{1,0:T(2,128)(2,1)S(1)}, u32[]{:S(2)}, u32[]{:S(2)}) collective-permute-start(bf16[2,768]{1,0:T(2,128)(2,1)S(1)} %get-tuple-element.83), channel_id=1, source_target_pairs={{2,0},{4,2},{6,4},{8,6},{10,8},{12,10},{14,12},{16,14},{18,16},{20... | collective-permute-start | bytes 9224 | tf_op jit(solution)/shard_map/ppermute | solution.py:25
  266.0 5.5 %collective-permute-start.3 = (bf16[2,768]{1,0:T(2,128)(2,1)S(1)}, bf16[2,768]{1,0:T(2,128)(2,1)S(1)}, u32[]{:S(2)}, u32[]{:S(2)}) collective-permute-start(bf16[2,768]{1,0:T(2,128)(2,1)S(1)} %get-tuple-element.82), channel_id=1, source_target_pairs={{0,2},{2,4},{4,6},{6,8},{8,10},{10,12},{12,14},{14,16},{16,18},{18... | collective-permute-start | bytes 9224 | tf_op jit(solution)/shard_map/ppermute | solution.py:23
  269.0 3.2 %slice-start.4 = ((s8[5898240]{0:T(1024)(128)(4,1)}), s8[1703936]{0:T(1024)(128)(4,1)S(1)}, s32[]{:S(2)}) async-start(s8[5898240]{0:T(1024)(128)(4,1)} %bitcast.122), calls=%async_computation.6 | async-start | bytes 3407872
  271.3 2.2 slice-start.5
Sparse Core Ops, SparseCore 0:
  124.9 53.7 reduce-scatter.1
where the time goes:
time: 288 us
  matrix products  98.3 us (34%)
  blocking collectives  91.2 us (32%)
  waiting for transfers between devices  55.3 us (19%)
  between operations  15.2 us (5%)
  other arithmetic  13.8 us (5%)
  starting transfers between devices  8.12 us (3%)
  local copies, waits for them, and re-layouts  5.34 us (2%)
    psum x1, blocking collectives, shards(): lax.psum(jnp.dot(member, projected, precision=highest), ('seq', 'col'))  57.6 us
    reduce_scatter x1, waiting for transfers between devices, shards(): lax.psum_scatter(placed, ('seq', 'col'), scatter_dimension=0, tiled=True)  54 us
    dot_general x4, matrix products, pair_step(): jnp.einsum('ijkl,jl->ik', outer_grad, right_wide, precision=highest)  41.7 us
    all_gather x1, blocking collectives, shards(): every = lax.all_gather(normed, ('seq', 'col'), axis=0, tiled=True)  25.4 us
    dot_general x4, matrix products, pair_step(): jnp.einsum('ijkl,ik->jl', outer_grad, rows_left, precision=highest)  18.9 us
    dot_general x1, matrix products, shards(): jnp.dot(unfolded, conv_weight, preferred_element_type=jnp.float32)  8.45 us
    psum x1, blocking collectives, shards(): center = lax.psum(unit, 'batch') / lax.axis_size('batch')  8.16 us
    dot_general x1, matrix products, shards(): jnp.einsum('tko,kio->ti', stacked, conv_weight.reshape(kernel, channels,...  7.36 us
  transfers between devices with their start and end apart: 5, of which 2 were waited for; matrix products, arithmetic and copies ran while one was open for 2% of the time, Pallas kernels for 0%

commit v1 on v0

v1 whole, which is shorter than its diff:
```python
import functools

import jax
import jax.numpy as jnp
from jax import lax
from jax.experimental import pallas as pl
from jax.experimental.pallas import tpu as pltpu
from jax.sharding import PartitionSpec as P

OP = 32
PATCH = 16
POOL = 128
BUCKETS = 32
BASES = 4
LANES = 128
PAD = 8

MESH = pl.DeviceIdType.MESH
F32 = jnp.float32
BF16 = jnp.bfloat16


def nn(a, b):
    return lax.dot_general(a, b, (((1,), (0,)), ((), ())), preferred_element_type=F32)


def nt(a, b):
    return lax.dot_general(a, b, (((1,), (1,)), ((), ())), preferred_element_type=F32)


def halves(values):
    upper = values.astype(BF16)
    lower = (values - upper.astype(F32)).astype(BF16)
    return jnp.concatenate([upper, lower], axis=0)


def joined(values):
    rows = values.shape[0] // 2
    return values[:rows] + values[rows:]


def iota(shape, dim):
    return lax.broadcasted_iota(jnp.int32, shape, dim)


def body(
    counts,
    tok,
    stem,
    bias,
    gain,
    pair,
    proj,
    buck,
    conv_h,
    up_h,
    outw_h,
    cot_h,
    out_h,
    emb,
    conv,
    up,
    outw,
    cot,
    grid,
    seen,
    hot,
    mixed,
    slope,
    pool,
    dpad,
    outv,
    halo_tok,
    lr,
    got_left,
    got_right,
    part_left,
    part_right,
    sum_left,
    sum_right,
    marks,
    sk,
    sk_a,
    sk_b,
    sk_bsrc,
    sk_c,
    sk_csrc,
    load_sem,
    store_sem,
    tok_send,
    tok_recv,
    left_send,
    left_recv,
    right_send,
    right_recv,
    gl_send,
    gl_recv,
    gr_send,
    gr_recv,
    edge_send,
    edge_recv,
    a_send,
    a_recv,
    b_send,
    b_recv,
    c_send,
    c_recv,
):
    seq_n, col_n, batch_n = counts
    seq, col, bat = lax.axis_index("seq"), lax.axis_index("col"), lax.axis_index("batch")
    me = seq * col_n + col
    last = seq_n * col_n - 1
    channels = conv.shape[1]
    kernel = conv.shape[0] // channels
    reach = (kernel - 1) // 2
    patches = slope.shape[0]
    bins = patches // POOL
    width = stem.shape[0]
    rows_n, cols_n = bins * col_n, bins * seq_n

    loads = [
        pltpu.make_async_copy(src, dst, load_sem.at[at])
        for at, (src, dst) in enumerate(((conv_h, conv), (up_h, up), (outw_h, outw), (cot_h, cot)))
    ]
    for load in loads:
        load.start()

    def place(linear):
        return {"seq": lax.div(linear, col_n), "col": lax.rem(linear, col_n), "batch": bat}

    def at(s, c, b):
        return {"seq": s, "col": c, "batch": b}

    def remote(src, dst, send, recv, device):
        return pltpu.make_async_remote_copy(
            src_ref=src,
            dst_ref=dst,
            send_sem=send,
            recv_sem=recv,
            device_id=device,
            device_id_type=MESH,
        )

    barrier = pltpu.get_barrier_semaphore()
    for step in range(1, seq_n * col_n):
        pl.semaphore_signal(
            barrier,
            inc=1,
            device_id=place(lax.rem(me + step, seq_n * col_n)),
            device_id_type=MESH,
        )
    for b_step in range(1, batch_n):
        for c_step in range(col_n):
            pl.semaphore_signal(
                barrier,
                inc=1,
                device_id=at(seq, lax.rem(col + c_step, col_n), lax.rem(bat + b_step, batch_n)),
                device_id_type=MESH,
            )

    spread = (lax.rem(iota((LANES, LANES), 0), PATCH) == lax.div(lax.rem(iota((LANES, LANES), 1), width), BASES)).astype(BF16)

    def expand(lines):
        count = lines.shape[0]
        wide = jnp.broadcast_to(lines.astype(F32)[:, None, :], (count, PAD, LANES)).reshape(count * PAD, LANES)
        own = lax.div(iota(wide.shape, 1), PATCH) == lax.rem(iota(wide.shape, 0), PAD)
        return nn(jnp.where(own, wide, 0.0).astype(BF16), spread)

    seen[pl.ds(PAD, patches), :] = expand(tok[...])
    mixed[pl.ds(kernel * width, width), :] = jnp.zeros((width, channels), BF16)

    pl.semaphore_wait(barrier, seq_n * col_n - 1 + (batch_n - 1) * col_n)

    lines_n = tok.shape[0]
    to_left = remote(tok.at[pl.ds(0, PAD)], halo_tok.at[1], tok_send.at[0], tok_recv.at[1], place(jnp.maximum(me - 1, 0)))
    to_right = remote(tok.at[pl.ds(lines_n - PAD, PAD)], halo_tok.at[0], tok_send.at[1], tok_recv.at[0], place(jnp.minimum(me + 1, last)))

    @pl.when(me > 0)
    def _():
        to_left.start()

    @pl.when(me < last)
    def _():
        to_right.start()

    loads[0].wait()
    for k in range(kernel):
        mixed[pl.ds(k * width, width), :] = nn(stem[...], conv[pl.ds(k * channels, channels), :]).astype(BF16)

    @pl.when(me > 0)
    def _():
        to_left.wait_send()
        to_right.wait_recv()
        seen[pl.ds(0, PAD), :] = expand(halo_tok[0, PAD - 1 : PAD, :])

    @pl.when(me == 0)
    def _():
        seen[pl.ds(0, PAD), :] = jnp.full((PAD, LANES), -1.0, F32)

    @pl.when(me < last)
    def _():
        to_right.wait_send()
        to_left.wait_recv()
        seen[pl.ds(PAD + patches, PAD), :] = expand(halo_tok[1, 0:1, :])

    @pl.when(me == last)
    def _():
        seen[pl.ds(PAD + patches, PAD), :] = jnp.full((PAD, LANES), -1.0, F32)

    lane = iota((patches, LANES), 1)
    base = lax.rem(lane, BASES).astype(F32)
    for group in range((kernel + 1) // 2):
        first = PAD - reach + 2 * group
        low = seen[pl.ds(first, patches), :]
        if 2 * group + 1 < kernel:
            high = seen[pl.ds(first + 1, patches), :]
        else:
            high = -1.0
        hot[:, group * LANES : (group + 1) * LANES] = jnp.where(jnp.where(lane < width, low, high) == base, 1.0, 0.0).astype(BF16)

    root = 0.7978845608028654
    cube = root * 0.044715

    @pl.loop(0, bins)
    def _(b):
        rows = pl.ds(pl.multiple_of(b * POOL, POOL), POOL)
        v = nn(hot[rows, :], mixed[...]) + bias[...]
        square = v * v
        t = jnp.tanh(v * (root + cube * square))
        half = 0.5 + 0.5 * t
        pool[pl.ds(b, 1), :] = jnp.sum(v * half, axis=0, keepdims=True) * (1.0 / POOL)
        slope[rows, :] = (half + 0.5 * v * (1.0 - t * t) * (root + 3.0 * cube * square)) * (1.0 / POOL)

    loads[1].wait()
    hidden = nn(pool[...].astype(BF16), up[...])
    inverse = lax.rsqrt(jnp.mean(hidden * hidden, axis=1, keepdims=True) + 1e-06)
    normed = (hidden * inverse * gain[...]).astype(BF16)
    lr[...] = jnp.zeros(lr.shape, F32)
    lr[:, : 2 * OP] = nn(normed, pair[...]).astype(BF16).astype(F32)

    user = lax.div(me, seq_n)
    slot = lax.rem(me, seq_n)
    lefts, rights = [], []
    for step in range(1, col_n):
        peer = lax.rem(col + step, col_n)
        lefts.append(remote(lr, got_left.at[col], left_send.at[step], left_recv.at[col], at(seq, peer, bat)))
        lefts[-1].start()
    for s in range(seq_n):
        copy = remote(lr, got_right.at[slot], right_send.at[s], right_recv.at[slot], at(s, user, bat))
        rights.append((copy, (seq != s) | (col != user)))

        @pl.when(rights[-1][1])
        def _():
            copy.start()

    got_left[col] = lr[...]

    @pl.when(col == user)
    def _():
        got_right[slot] = lr[...]

    loads[2].wait()
    loads[3].wait()
    step_rows = 2 * LANES

    @pl.loop(0, rows_n * cols_n // step_rows)
    def _(i):
        rows = pl.ds(pl.multiple_of(i * step_rows, step_rows), step_rows)
        grid[rows, :] = nt(cot[rows, :], outw[...])

    for step in range(1, col_n):
        peer = lax.rem(col + step, col_n)
        remote(lr, got_left.at[peer], left_send.at[step], left_recv.at[peer], at(seq, peer, bat)).wait_recv()
    for s in range(seq_n):
        owner = col * seq_n + s

        @pl.when(owner != me)
        def _():
            remote(lr, got_right.at[s], right_send.at[s], right_recv.at[s], place(owner)).wait_recv()

    for copy in lefts:
        copy.wait_send()
    for copy, other in rights:

        @pl.when(other)
        def _():
            copy.wait_send()

    outer = OP * OP
    pick_left = (iota((LANES, outer), 0) == lax.div(iota((LANES, outer), 1), OP)).astype(BF16)
    pick_right = (iota((LANES, outer), 0) == OP + lax.rem(iota((LANES, outer), 1), OP)).astype(BF16)
    wide_left = nn(got_left[...].reshape(rows_n, LANES).astype(BF16), pick_left)
    wide_right = nn(got_right[...].reshape(cols_n, LANES).astype(BF16), pick_right)
    over_cols, over_rows = [], []
    for tile in range(outer // LANES):
        lanes = slice(tile * LANES, (tile + 1) * LANES)
        cells = grid[:, lanes].reshape(rows_n, cols_n, LANES)
        over_cols.append(jnp.sum(cells * wide_right[None, :, lanes], axis=1))
        over_rows.append(jnp.sum(cells * wide_left[:, None, lanes], axis=0))
    part_left[...] = joined(nt(halves(jnp.concatenate(over_cols, axis=1)), pick_left))
    part_right[...] = joined(nt(halves(jnp.concatenate(over_rows, axis=1)), pick_right))

    lefts, rights = [], []
    for step in range(1, col_n):
        peer = lax.rem(col + step, col_n)
        piece = part_left.at[pl.ds(pl.multiple_of(peer * bins, bins), bins)]
        lefts.append(remote(piece, sum_left.at[col], gl_send.at[step], gl_recv.at[col], at(seq, peer, bat)))
        lefts[-1].start()
    for s in range(seq_n):
        owner = col * seq_n + s
        copy = remote(part_right.at[pl.ds(s * bins, bins)], sum_right.at[seq], gr_send.at[s], gr_recv.at[seq], place(owner))
        rights.append((copy, owner != me))

        @pl.when(owner != me)
        def _():
            copy.start()

        @pl.when(owner == me)
        def _():
            sum_right[seq] = part_right[s * bins : (s + 1) * bins, :]

    sum_left[col] = part_left[pl.ds(pl.multiple_of(col * bins, bins), bins), :]

    member = (buck[...] == iota((BUCKETS, kernel * channels), 0)).astype(BF16)
    stems = [nt(member[:, k * channels : (k + 1) * channels], stem[...]) for k in range(kernel)]
    stems.append(jnp.zeros((BUCKETS, width), F32))
    marks[...] = halves(joined(nt(halves(jnp.concatenate(stems, axis=1)), hot[...])))

    for step in range(1, col_n):
        peer = lax.rem(col + step, col_n)
        remote(lr, sum_left.at[peer], gl_send.at[step], gl_recv.at[peer], at(seq, peer, bat)).wait_recv()
    for s in range(seq_n):

        @pl.when((seq != s) | (col != user))
        def _():
            remote(lr, sum_right.at[s], gr_send.at[s], gr_recv.at[s], at(s, user, bat)).wait_recv()

    both = jnp.sum(sum_left[...], axis=0) + jnp.sum(sum_right[...], axis=0)
    d_normed = joined(nt(halves(both[:, : 2 * OP]), pair[...]))
    scaled = d_normed * gain[...]
    inner = jnp.mean(scaled * hidden, axis=1, keepdims=True)
    d_hidden = inverse * scaled - hidden * (inverse * inverse * inverse) * inner
    pool[...] = joined(nt(halves(d_hidden), up[...]))

    dpad[pl.ds(PAD, PAD), :] = slope[:PAD, :] * pool[0:1, :]
    dpad[pl.ds(patches, PAD), :] = slope[patches - PAD :, :] * pool[bins - 1 : bins, :]
    edge_left = remote(dpad.at[pl.ds(PAD, PAD)], dpad.at[pl.ds(PAD + patches, PAD)], edge_send.at[0], edge_recv.at[1], place(jnp.maximum(me - 1, 0)))
    edge_right = remote(dpad.at[pl.ds(patches, PAD)], dpad.at[pl.ds(0, PAD)], edge_send.at[1], edge_recv.at[0], place(jnp.minimum(me + 1, last)))

    @pl.when(me > 0)
    def _():
        edge_left.start()

    @pl.when(me < last)
    def _():
        edge_right.start()

    @pl.when(me == 0)
    def _():
        dpad[pl.ds(0, PAD), :] = jnp.zeros((PAD, channels), F32)

    @pl.when(me == last)
    def _():
        dpad[pl.ds(PAD + patches, PAD), :] = jnp.zeros((PAD, channels), F32)

    for copy in lefts:
        copy.wait_send()
    for copy, other in rights:

        @pl.when(other)
        def _():
            copy.wait_send()

    total = jnp.zeros((2 * BUCKETS, channels), F32)
    for b in range(bins):
        first = b * POOL
        cells = slope[first : first + POOL, :] * pool[b : b + 1, :]
        low = PAD if b == 0 else 0
        high = POOL - PAD if b == bins - 1 else POOL
        dpad[pl.ds(PAD + first + low, high - low), :] = cells[low:high]
        total = total + nn(marks[:, first : first + POOL], cells.astype(BF16))
    sk[...] = lax.dot_general(
        joined(total), proj[...], (((1,), (0,)), ((), ())), precision=lax.Precision.HIGHEST, preferred_element_type=F32
    )
    share = BUCKETS // col_n

    sends_a = []
    for step in range(1, col_n):
        peer = lax.rem(col + step, col_n)
        piece = sk.at[pl.ds(pl.multiple_of(peer * share, share), share)]
        sends_a.append(remote(piece, sk_a.at[col], a_send.at[step], a_recv.at[col], at(seq, peer, bat)))
        sends_a[-1].start()
    sk_a[col] = sk[pl.ds(pl.multiple_of(col * share, share), share), :]
    sends_b = [
        remote(sk_bsrc, sk_b.at[seq], b_send.at[step], b_recv.at[seq], at(lax.rem(seq + step, seq_n), col, bat))
        for step in range(1, seq_n)
    ]
    pairs = [(b, c) for b in range(batch_n) for c in range(col_n) if b + c > 0]
    sends_c = [
        remote(
            sk_csrc,
            sk_c.at[bat, col],
            c_send.at[b, c],
            c_recv.at[bat, col],
            at(seq, lax.rem(col + c, col_n), lax.rem(bat + b, batch_n)),
        )
        for b, c in pairs
    ]

    chunk = 2 * LANES
    chunks = patches // chunk

    @pl.loop(0, chunks)
    def _(i):
        @pl.when(i == 1)
        def _():
            for step in range(1, col_n):
                peer = lax.rem(col + step, col_n)
                remote(sk_bsrc, sk_a.at[peer], a_send.at[step], a_recv.at[peer], at(seq, peer, bat)).wait_recv()
            sk_bsrc[...] = jnp.sum(sk_a[...], axis=0)
            sk_b[seq] = jnp.sum(sk_a[...], axis=0)
            for copy in sends_b:
                copy.start()

        @pl.when(i == 2)
        def _():
            for step in range(1, seq_n):
                peer = lax.rem(seq + step, seq_n)
                remote(sk_bsrc, sk_b.at[peer], b_send.at[step], b_recv.at[peer], at(peer, col, bat)).wait_recv()
            sk_csrc[...] = jnp.sum(sk_b[...], axis=0)
            sk_c[bat, col] = jnp.sum(sk_b[...], axis=0)
            for copy in sends_c:
                copy.start()

            @pl.when(me > 0)
            def _():
                edge_left.wait_send()
                edge_right.wait_recv()

            @pl.when(me < last)
            def _():
                edge_right.wait_send()
                edge_left.wait_recv()

        spot = lax.rem(i + 1, chunks)
        begin = pl.multiple_of(spot * chunk, chunk)
        wide = dpad[pl.ds(begin, chunk + 2 * PAD), :]
        acc = jnp.zeros((chunk, channels), F32)
        for k in range(kernel):
            shift = PAD + reach - k
            acc = acc + nt(wide[shift : shift + chunk].astype(BF16), conv[pl.ds(k * channels, channels), :])
        outv[pl.ds(begin, chunk), :] = acc.astype(BF16)
        pltpu.make_async_copy(outv.at[pl.ds(begin, chunk)], out_h.at[pl.ds(begin, chunk)], store_sem.at[spot]).start()

    for b, c in pairs:
        other_b, other_c = lax.rem(bat + b, batch_n), lax.rem(col + c, col_n)
        remote(sk_csrc, sk_c.at[other_b, other_c], c_send.at[b, c], c_recv.at[other_b, other_c], at(seq, other_c, other_b)).wait_recv()

    def unit(values):
        values = values.reshape(BUCKETS, values.shape[-1])
        return values * lax.rsqrt(jnp.mean(values * values) + 1e-06)

    center = unit(sk_c[0])
    for b in range(1, batch_n):
        center = center + unit(sk_c[b])
    emb[...] = unit(sk_c[bat]) - center * (1.0 / batch_n)
    for copy in sends_a + sends_b + sends_c:
        copy.wait_send()
    for i in range(chunks):
        rows = pl.ds(i * chunk, chunk)
        pltpu.make_async_copy(outv.at[rows], out_h.at[rows], store_sem.at[i]).wait()


def shards(
    tokens,
    stem_weight,
    conv_weight,
    conv_bias,
    up_weight,
    norm_gain,
    pair_weight,
    out_weight,
    cotangent,
    projection,
    buckets,
):
    seq_n, col_n, batch_n = (lax.axis_size(axis) for axis in ("seq", "col", "batch"))
    channels = conv_weight.shape[1]
    kernel = conv_weight.shape[0] // channels
    patches = tokens.shape[1] // PATCH
    bins = patches // POOL
    rows_n, cols_n = bins * col_n, bins * seq_n
    proj_n = projection.shape[1]
    share = BUCKETS // col_n
    hot_n = (kernel + 1) // 2 * LANES
    vmem = pl.BlockSpec(memory_space=pltpu.VMEM)
    hbm = pl.BlockSpec(memory_space=pl.ANY)
    dma = pltpu.SemaphoreType.DMA
    cot = cotangent.reshape(rows_n * cols_n, cotangent.shape[3])
    scratch = [
        pltpu.VMEM(conv_weight.shape, BF16),
        pltpu.VMEM(up_weight.shape, BF16),
        pltpu.VMEM(out_weight.shape, BF16),
        pltpu.VMEM(cot.shape, BF16),
        pltpu.VMEM((rows_n * cols_n, OP * OP), F32),
        pltpu.VMEM((patches + 2 * PAD, LANES), F32),
        pltpu.VMEM((patches, hot_n), BF16),
        pltpu.VMEM((hot_n, channels), BF16),
        pltpu.VMEM((patches, channels), F32),
        pltpu.VMEM((bins, channels), F32),
        pltpu.VMEM((patches + 2 * PAD, channels), F32),
        pltpu.VMEM((patches, channels), BF16),
        pltpu.VMEM((2, PAD, LANES), jnp.int32),
        pltpu.VMEM((bins, LANES), F32),
        pltpu.VMEM((col_n, bins, LANES), F32),
        pltpu.VMEM((seq_n, bins, LANES), F32),
        pltpu.VMEM((rows_n, LANES), F32),
        pltpu.VMEM((cols_n, LANES), F32),
        pltpu.VMEM((col_n, bins, LANES), F32),
        pltpu.VMEM((seq_n, bins, LANES), F32),
        pltpu.VMEM((2 * BUCKETS, patches), BF16),
        pltpu.VMEM((BUCKETS, proj_n), F32),
        pltpu.VMEM((col_n, share, proj_n), F32),
        pltpu.VMEM((seq_n, share, proj_n), F32),
        pltpu.VMEM((share, proj_n), F32),
        pltpu.VMEM((batch_n, col_n, share, proj_n), F32),
        pltpu.VMEM((share, proj_n), F32),
        dma((4,)),
        dma((patches // (2 * LANES),)),
        dma((2,)),
        dma((2,)),
        dma((col_n,)),
        dma((col_n,)),
        dma((seq_n,)),
        dma((seq_n,)),
        dma((col_n,)),
        dma((col_n,)),
        dma((seq_n,)),
        dma((seq_n,)),
        dma((2,)),
        dma((2,)),
        dma((col_n,)),
        dma((col_n,)),
        dma((seq_n,)),
        dma((seq_n,)),
        dma((batch_n, col_n)),
        dma((batch_n, col_n)),
    ]
    input_grad, embedding = pl.pallas_call(
        functools.partial(body, (seq_n, col_n, batch_n)),
        out_shape=(
            jax.ShapeDtypeStruct((patches, channels), BF16),
            jax.ShapeDtypeStruct((BUCKETS, proj_n), F32),
        ),
        in_specs=[vmem] * 7 + [hbm] * 4,
        out_specs=(hbm, vmem),
        scratch_shapes=scratch,
        compiler_params=pltpu.CompilerParams(
            collective_id=0, has_side_effects=True, vmem_limit_bytes=56 * 2**20
        ),
    )(
        tokens.reshape(patches * PATCH // LANES, LANES),
        stem_weight,
        conv_bias.reshape(1, channels),
        norm_gain.reshape(1, -1),
        pair_weight,
        projection,
        buckets.reshape(1, -1),
        conv_weight,
        up_weight,
        out_weight,
        cot,
    )
    return (input_grad[None], embedding[None])


def solution(mesh):
    in_specs = (
        P("batch", ("seq", "col")),
        P(),
        P(),
        P(),
        P(),
        P(),
        P(),
        P(),
        P("batch", "seq", "col", None),
        P(),
        P(),
    )
    out_specs = (P("batch", ("seq", "col"), None), P("batch", None, None))
    return jax.shard_map(shards, mesh=mesh, in_specs=in_specs, out_specs=out_specs, check_vma=False)
```

time: 288 us -> 45.7 us (0.16)
  matrix products: 98.3 us -> 0 us
  blocking collectives: 91.2 us -> 0 us
  waiting for transfers between devices: 55.3 us -> 0 us
  Pallas kernels: 0 us -> 35.6 us
  between operations: 15.2 us -> 0.65 us
  other arithmetic: 13.8 us -> 0 us
  starting transfers between devices: 8.12 us -> 0 us
  local copies, waits for them, and re-layouts: 5.34 us -> 9.01 us
    dot_general x26 -> x0, matrix products: 98.3 us -> none  [the longest x4 41.7 us: pair_step(): jnp.einsum('ijkl,jl->ik', outer_grad, right_wide, precision=highest)]
    psum x2 -> x0, blocking collectives: 65.8 us -> none  [the longest x1 57.6 us: shards(): lax.psum(jnp.dot(member, projected, precision=highest), ('seq', 'col'))]
    reduce_scatter x1 -> x0, waiting for transfers between devices: 54 us -> none  [shards(): lax.psum_scatter(placed, ('seq', 'col'), scatter_dimension=0, tiled=True)]
    pallas_call x0 -> x1, Pallas kernels: none -> 35.6 us  [shards(): pl.pallas_call(functools.partial(body, (seq_n, col_n, batch_n)), out_shap...]
    all_gather x1 -> x0, blocking collectives: 25.4 us -> none  [shards(): every = lax.all_gather(normed, ('seq', 'col'), axis=0, tiled=True)]
    ppermute x4 -> x0, starting transfers between devices: 8.08 us -> none  [the longest x2 5.38 us: extended(): lax.ppermute(tail, axis, [(i, (i + 1) % count) for i in range(ends)])]
    unnamed x11 -> x0, other arithmetic: 7.13 us -> none
    reshape x0 -> x3, local copies, waits for them, and re-layouts: none -> 3.89 us  [the longest x1 1.33 us: shards(): buckets.reshape(1, -1)]
  transfers between devices with their start and end apart: 5 -> 0, of which waited for: 2 -> 0; matrix products, arithmetic and copies ran while one was open for 2% -> 0% of each run, Pallas kernels for 0% -> 0%
where the time goes in v1:
time: 45.7 us; the launch traced here: 45.3 us
  Pallas kernels  35.6 us (78%)
  local copies, waits for them, and re-layouts  9.01 us (20%)
  between operations  0.65 us (1%)
    pallas_call x1, Pallas kernels, shards(): pl.pallas_call(functools.partial(body, (seq_n, col_n, batch_n)), out_shap...  35.6 us
    unnamed x5, local copies, waits for them, and re-layouts  5.11 us
    reshape x1, local copies, waits for them, and re-layouts, shards(): buckets.reshape(1, -1)  1.33 us
    reshape x1, local copies, waits for them, and re-layouts, shards(): norm_gain.reshape(1, -1)  1.29 us
    reshape x1, local copies, waits for them, and re-layouts, shards(): conv_bias.reshape(1, channels)  1.27 us

profile of v1, /device:TPU:0, one launch (start us, length us, event | category | flops | bytes accessed | tf_op | source)
XLA Modules:
  0.0 45.3 jit_solution(16970665158622035197)
XLA Ops:
  0.6 1.3 %reshape.20.bias = f32[1,768]{1,0:T(1,128)} reshape(f32[768]{0:T(1024)} %param.14) | data formatting | bytes 6144 | tf_op jit(solution)/shard_map/reshape | solution.py:564
  1.9 1.3 %reshape.21.gain = f32[1,1536]{1,0:T(1,128)} reshape(f32[1536]{0:T(1024)} %param.16) | data formatting | bytes 12288 | tf_op jit(solution)/shard_map/reshape | solution.py:565
  3.2 1.3 %reshape.22.buck = s32[1,3840]{1,0:T(1,128)} reshape(s32[3840]{0:T(1024)} %param.21) | data formatting | bytes 30720 | tf_op jit(solution)/shard_map/reshape | solution.py:568
  4.5 1.8 %copy.13.pair = bf16[1536,64]{1,0:T(8,128)(2,1)} copy(bf16[1536,64]{0,1:T(8,128)(2,1)} %param.17) | data formatting | bytes 393216 | tf_op args[6]
  6.4 35.6 %shard_map.122 = (bf16[1024,768]{1,0:T(8,128)(2,1)}, f32[32,128]{1,0:T(8,128)}) custom-call(s32[128,128]{1,0:T(8,128)} %bitcast.6, bf16[64,768]{1,0:T(8,128)(2,1)} %stem.1, f32[1,768]{1,0:T(1,128)} %reshape.20.bias, f32[1,1536]{1,0:T(1,128)} %reshape.21.gain, bf16[1536,64]{1,0:T(8,128)(2,1)} %copy.13.pair, f32[768,128]{1,0:T(8,128)} %proj.1, ...), custom_call_target="tpu_custom_call" | custom-call | tf_op jit(solution)/shard_map/pallas_call | solution.py:549
  42.0 0.0 copy-start
  42.0 2.7 %copy.16 = bf16[1,1024,768]{2,1,0:T(8,128)(2,1)} copy(bf16[1,1024,768]{2,1,0:T(8,128)(2,1)} %bitcast.4) | data formatting | bytes 3145728
  44.7 0.0 copy-done
  44.7 0.6 %copy.17 = f32[1,32,128]{2,1,0:T(8,128)} copy(f32[1,32,128]{2,1,0:T(8,128)S(1)} %bitcast.7) | data formatting | bytes 32768
Async XLA Ops:
  42.0 2.7 %copy-start = (f32[32,128]{1,0:T(8,128)S(1)}, f32[32,128]{1,0:T(8,128)}, u32[]{:S(2)}) copy-start(f32[32,128]{1,0:T(8,128)} %get-tuple-element.5) | copy-start | bytes 49156

commit v2 on v1

--- a/solution.py
+++ b/solution.py
@@ -45,6 +45,19 @@
 
 def body(
     counts,
+    tok_h,
+    stem_h,
+    bias_h,
+    gain_h,
+    pair_h,
+    proj_h,
+    buck_h,
+    conv_h,
+    up_h,
+    outw_h,
+    cot_h,
+    out_h,
+    emb,
     tok,
     stem,
     bias,
@@ -52,12 +65,6 @@
     pair,
     proj,
     buck,
-    conv_h,
-    up_h,
-    outw_h,
-    cot_h,
-    out_h,
-    emb,
     conv,
     up,
     outw,
@@ -118,12 +125,17 @@
     width = stem.shape[0]
     rows_n, cols_n = bins * col_n, bins * seq_n
 
-    loads = [
-        pltpu.make_async_copy(src, dst, load_sem.at[at])
-        for at, (src, dst) in enumerate(((conv_h, conv), (up_h, up), (outw_h, outw), (cot_h, cot)))
-    ]
+    taps = [pl.ds(k * channels, channels) for k in range(kernel)]
+    moves = [(tok_h, tok), (stem_h, stem)]
+    moves += [(conv_h.at[tap], conv.at[tap]) for tap in taps]
+    moves += [(bias_h, bias), (up_h, up), (gain_h, gain), (pair_h, pair)]
+    moves += [(outw_h, outw), (cot_h, cot), (buck_h, buck), (proj_h, proj)]
+    loads = [pltpu.make_async_copy(src, dst, load_sem.at[at]) for at, (src, dst) in enumerate(moves)]
     for load in loads:
         load.start()
+    load_tok, load_stem = loads[:2]
+    load_conv = loads[2 : 2 + kernel]
+    load_bias, load_up, load_gain, load_pair, load_outw, load_cot, load_buck, load_proj = loads[2 + kernel :]
 
     def place(linear):
         return {"seq": lax.div(linear, col_n), "col": lax.rem(linear, col_n), "batch": bat}
@@ -166,6 +178,7 @@
         own = lax.div(iota(wide.shape, 1), PATCH) == lax.rem(iota(wide.shape, 0), PAD)
         return nn(jnp.where(own, wide, 0.0).astype(BF16), spread)
 
+    load_tok.wait()
     seen[pl.ds(PAD, patches), :] = expand(tok[...])
     mixed[pl.ds(kernel * width, width), :] = jnp.zeros((width, channels), BF16)
 
@@ -183,8 +196,9 @@
     def _():
         to_right.start()
 
-    loads[0].wait()
+    load_stem.wait()
     for k in range(kernel):
+        load_conv[k].wait()
         mixed[pl.ds(k * width, width), :] = nn(stem[...], conv[pl.ds(k * channels, channels), :]).astype(BF16)
 
     @pl.when(me > 0)
@@ -221,22 +235,27 @@
     root = 0.7978845608028654
     cube = root * 0.044715
 
+    load_bias.wait()
+    shift_row = bias[...][None, :]
+
     @pl.loop(0, bins)
     def _(b):
         rows = pl.ds(pl.multiple_of(b * POOL, POOL), POOL)
-        v = nn(hot[rows, :], mixed[...]) + bias[...]
+        v = nn(hot[rows, :], mixed[...]) + shift_row
         square = v * v
         t = jnp.tanh(v * (root + cube * square))
         half = 0.5 + 0.5 * t
         pool[pl.ds(b, 1), :] = jnp.sum(v * half, axis=0, keepdims=True) * (1.0 / POOL)
         slope[rows, :] = (half + 0.5 * v * (1.0 - t * t) * (root + 3.0 * cube * square)) * (1.0 / POOL)
 
-    loads[1].wait()
+    for load in (load_up, load_gain, load_pair):
+        load.wait()
+    gain_row = gain[...][None, :]
     hidden = nn(pool[...].astype(BF16), up[...])
     inverse = lax.rsqrt(jnp.mean(hidden * hidden, axis=1, keepdims=True) + 1e-06)
-    normed = (hidden * inverse * gain[...]).astype(BF16)
+    normed = (hidden * inverse * gain_row).astype(BF16)
     lr[...] = jnp.zeros(lr.shape, F32)
-    lr[:, : 2 * OP] = nn(normed, pair[...]).astype(BF16).astype(F32)
+    lr[:, : 2 * OP] = nt(normed, pair[...]).astype(BF16).astype(F32)
 
     user = lax.div(me, seq_n)
     slot = lax.rem(me, seq_n)
@@ -259,8 +278,8 @@
     def _():
         got_right[slot] = lr[...]
 
-    loads[2].wait()
-    loads[3].wait()
+    load_outw.wait()
+    load_cot.wait()
     step_rows = 2 * LANES
 
     @pl.loop(0, rows_n * cols_n // step_rows)
@@ -321,7 +340,8 @@
 
     sum_left[col] = part_left[pl.ds(pl.multiple_of(col * bins, bins), bins), :]
 
-    member = (buck[...] == iota((BUCKETS, kernel * channels), 0)).astype(BF16)
+    load_buck.wait()
+    member = (buck[...][None, :] == iota((BUCKETS, kernel * channels), 0)).astype(BF16)
     stems = [nt(member[:, k * channels : (k + 1) * channels], stem[...]) for k in range(kernel)]
     stems.append(jnp.zeros((BUCKETS, width), F32))
     marks[...] = halves(joined(nt(halves(jnp.concatenate(stems, axis=1)), hot[...])))
@@ -336,8 +356,8 @@
             remote(lr, sum_right.at[s], gr_send.at[s], gr_recv.at[s], at(s, user, bat)).wait_recv()
 
     both = jnp.sum(sum_left[...], axis=0) + jnp.sum(sum_right[...], axis=0)
-    d_normed = joined(nt(halves(both[:, : 2 * OP]), pair[...]))
-    scaled = d_normed * gain[...]
+    d_normed = joined(nn(halves(both[:, : 2 * OP]), pair[...]))
+    scaled = d_normed * gain_row
     inner = jnp.mean(scaled * hidden, axis=1, keepdims=True)
     d_hidden = inverse * scaled - hidden * (inverse * inverse * inverse) * inner
     pool[...] = joined(nt(halves(d_hidden), up[...]))
@@ -379,6 +399,7 @@
         high = POOL - PAD if b == bins - 1 else POOL
         dpad[pl.ds(PAD + first + low, high - low), :] = cells[low:high]
         total = total + nn(marks[:, first : first + POOL], cells.astype(BF16))
+    load_proj.wait()
     sk[...] = lax.dot_general(
         joined(total), proj[...], (((1,), (0,)), ((), ())), precision=lax.Precision.HIGHEST, preferred_element_type=F32
     )
@@ -498,6 +519,13 @@
     dma = pltpu.SemaphoreType.DMA
     cot = cotangent.reshape(rows_n * cols_n, cotangent.shape[3])
     scratch = [
+        pltpu.VMEM((patches * PATCH // LANES, LANES), jnp.int32),
+        pltpu.VMEM(stem_weight.shape, BF16),
+        pltpu.VMEM(conv_bias.shape, F32),
+        pltpu.VMEM(norm_gain.shape, F32),
+        pltpu.VMEM(pair_weight.shape[::-1], BF16),
+        pltpu.VMEM(projection.shape, F32),
+        pltpu.VMEM(buckets.shape, jnp.int32),
         pltpu.VMEM(conv_weight.shape, BF16),
         pltpu.VMEM(up_weight.shape, BF16),
         pltpu.VMEM(out_weight.shape, BF16),
@@ -525,7 +553,7 @@
         pltpu.VMEM((share, proj_n), F32),
         pltpu.VMEM((batch_n, col_n, share, proj_n), F32),
         pltpu.VMEM((share, proj_n), F32),
-        dma((4,)),
+        dma((10 + kernel,)),
         dma((patches // (2 * LANES),)),
         dma((2,)),
         dma((2,)),
@@ -552,7 +580,7 @@
             jax.ShapeDtypeStruct((patches, channels), BF16),
             jax.ShapeDtypeStruct((BUCKETS, proj_n), F32),
         ),
-        in_specs=[vmem] * 7 + [hbm] * 4,
+        in_specs=[hbm] * 11,
         out_specs=(hbm, vmem),
         scratch_shapes=scratch,
         compiler_params=pltpu.CompilerParams(
@@ -561,11 +589,11 @@
     )(
         tokens.reshape(patches * PATCH // LANES, LANES),
         stem_weight,
-        conv_bias.reshape(1, channels),
-        norm_gain.reshape(1, -1),
-        pair_weight,
+        conv_bias,
+        norm_gain,
+        pair_weight.T,
         projection,
-        buckets.reshape(1, -1),
+        buckets,
         conv_weight,
         up_weight,
         out_weight,

time: 45.7 us -> 38.8 us (0.85)
  local copies, waits for them, and re-layouts: 9.01 us -> 3.27 us
  Pallas kernels: 35.6 us -> 34.7 us
    reshape x3 -> x0, local copies, waits for them, and re-layouts: 3.89 us -> none  [the longest x1 1.33 us: shards(): buckets.reshape(1, -1)]
    unnamed x5 -> x4, local copies, waits for them, and re-layouts: 5.11 us -> 3.27 us
    pallas_call x1, Pallas kernels: 35.6 us -> 34.7 us  [shards(): pl.pallas_call(functools.partial(body, (seq_n, col_n, batch_n)), out_shap...]
where the time goes in v2:
time: 38.8 us; the launch traced here: 38.6 us
  Pallas kernels  34.7 us (89%)
  local copies, waits for them, and re-layouts  3.27 us (8%)
  between operations  0.65 us (2%)
    pallas_call x1, Pallas kernels, shards(): pl.pallas_call(functools.partial(body, (seq_n, col_n, batch_n)), out_shap...  34.7 us
    unnamed x4, local copies, waits for them, and re-layouts  3.27 us

profile of v2, /device:TPU:0, one launch (start us, length us, event | category | flops | bytes accessed | tf_op | source)
XLA Modules:
  0.0 38.6 jit_solution(9851472083621967451)
XLA Ops:
  0.6 34.7 %shard_map.122 = (bf16[1024,768]{1,0:T(8,128)(2,1)}, f32[32,128]{1,0:T(8,128)}) custom-call(s32[128,128]{1,0:T(8,128)} %bitcast.8, bf16[64,768]{1,0:T(8,128)(2,1)} %stem_h.1, f32[768]{0:T(1024)} %bias_h.1, f32[1536]{0:T(1024)} %gain_h.1, bf16[64,1536]{1,0:T(8,128)(2,1)} %bitcast.7, f32[768,128]{1,0:T(8,128)} %proj_h.1, s32[3840]{0:T(1024)} %buck_h.1, ...), custom_call_target="tpu_custom_call" | custom-call | tf_op jit(solution)/shard_map/pallas_call | solution.py:577
  35.3 0.0 copy-start
  35.3 2.7 %copy.15 = bf16[1,1024,768]{2,1,0:T(8,128)(2,1)} copy(bf16[1,1024,768]{2,1,0:T(8,128)(2,1)} %bitcast.5) | data formatting | bytes 3145728
  38.0 0.0 copy-done
  38.0 0.6 %copy.16 = f32[1,32,128]{2,1,0:T(8,128)} copy(f32[1,32,128]{2,1,0:T(8,128)S(1)} %bitcast.9) | data formatting | bytes 32768
Async XLA Ops:
  35.3 2.7 %copy-start = (f32[32,128]{1,0:T(8,128)S(1)}, f32[32,128]{1,0:T(8,128)}, u32[]{:S(2)}) copy-start(f32[32,128]{1,0:T(8,128)} %get-tuple-element.5) | copy-start | bytes 49156

commit v3 on v2

--- a/solution.py
+++ b/solution.py
@@ -126,16 +126,15 @@
     rows_n, cols_n = bins * col_n, bins * seq_n
 
     taps = [pl.ds(k * channels, channels) for k in range(kernel)]
-    moves = [(tok_h, tok), (stem_h, stem)]
+    moves = [(tok_h, tok), (stem_h, stem), (buck_h, buck), (outw_h, outw), (cot_h, cot)]
     moves += [(conv_h.at[tap], conv.at[tap]) for tap in taps]
-    moves += [(bias_h, bias), (up_h, up), (gain_h, gain), (pair_h, pair)]
-    moves += [(outw_h, outw), (cot_h, cot), (buck_h, buck), (proj_h, proj)]
+    moves += [(bias_h, bias), (up_h, up), (gain_h, gain), (pair_h, pair), (proj_h, proj)]
     loads = [pltpu.make_async_copy(src, dst, load_sem.at[at]) for at, (src, dst) in enumerate(moves)]
     for load in loads:
         load.start()
-    load_tok, load_stem = loads[:2]
-    load_conv = loads[2 : 2 + kernel]
-    load_bias, load_up, load_gain, load_pair, load_outw, load_cot, load_buck, load_proj = loads[2 + kernel :]
+    load_tok, load_stem, load_buck, load_outw, load_cot = loads[:5]
+    load_conv = loads[5 : 5 + kernel]
+    load_bias, load_up, load_gain, load_pair, load_proj = loads[5 + kernel :]
 
     def place(linear):
         return {"seq": lax.div(linear, col_n), "col": lax.rem(linear, col_n), "batch": bat}
@@ -182,6 +181,22 @@
     seen[pl.ds(PAD, patches), :] = expand(tok[...])
     mixed[pl.ds(kernel * width, width), :] = jnp.zeros((width, channels), BF16)
 
+    load_stem.wait()
+    load_buck.wait()
+    member = (buck[...][None, :] == iota((BUCKETS, kernel * channels), 0)).astype(BF16)
+    stems = [nt(member[:, k * channels : (k + 1) * channels], stem[...]) for k in range(kernel)]
+    stems.append(jnp.zeros((BUCKETS, width), F32))
+    stem_marks = halves(jnp.concatenate(stems, axis=1))
+
+    load_outw.wait()
+    load_cot.wait()
+    step_rows = 2 * LANES
+
+    @pl.loop(0, rows_n * cols_n // step_rows)
+    def _(i):
+        rows = pl.ds(pl.multiple_of(i * step_rows, step_rows), step_rows)
+        grid[rows, :] = nt(cot[rows, :], outw[...])
+
     pl.semaphore_wait(barrier, seq_n * col_n - 1 + (batch_n - 1) * col_n)
 
     lines_n = tok.shape[0]
@@ -196,50 +211,29 @@
     def _():
         to_right.start()
 
-    load_stem.wait()
     for k in range(kernel):
         load_conv[k].wait()
         mixed[pl.ds(k * width, width), :] = nn(stem[...], conv[pl.ds(k * channels, channels), :]).astype(BF16)
 
-    @pl.when(me > 0)
-    def _():
-        to_left.wait_send()
-        to_right.wait_recv()
-        seen[pl.ds(0, PAD), :] = expand(halo_tok[0, PAD - 1 : PAD, :])
-
-    @pl.when(me == 0)
-    def _():
-        seen[pl.ds(0, PAD), :] = jnp.full((PAD, LANES), -1.0, F32)
-
-    @pl.when(me < last)
-    def _():
-        to_right.wait_send()
-        to_left.wait_recv()
-        seen[pl.ds(PAD + patches, PAD), :] = expand(halo_tok[1, 0:1, :])
-
-    @pl.when(me == last)
-    def _():
-        seen[pl.ds(PAD + patches, PAD), :] = jnp.full((PAD, LANES), -1.0, F32)
-
-    lane = iota((patches, LANES), 1)
-    base = lax.rem(lane, BASES).astype(F32)
-    for group in range((kernel + 1) // 2):
-        first = PAD - reach + 2 * group
-        low = seen[pl.ds(first, patches), :]
-        if 2 * group + 1 < kernel:
-            high = seen[pl.ds(first + 1, patches), :]
-        else:
-            high = -1.0
-        hot[:, group * LANES : (group + 1) * LANES] = jnp.where(jnp.where(lane < width, low, high) == base, 1.0, 0.0).astype(BF16)
+    def encode(first, count):
+        lane = iota((count, LANES), 1)
+        base = lax.rem(lane, BASES).astype(F32)
+        for group in range((kernel + 1) // 2):
+            spot = first + PAD - reach + 2 * group
+            low = seen[pl.ds(spot, count), :]
+            if 2 * group + 1 < kernel:
+                high = seen[pl.ds(spot + 1, count), :]
+            else:
+                high = -1.0
+            match = jnp.where(lane < width, low, high) == base
+            hot[first : first + count, group * LANES : (group + 1) * LANES] = jnp.where(match, 1.0, 0.0).astype(BF16)
 
     root = 0.7978845608028654
     cube = root * 0.044715
-
     load_bias.wait()
     shift_row = bias[...][None, :]
 
-    @pl.loop(0, bins)
-    def _(b):
+    def forward(b):
         rows = pl.ds(pl.multiple_of(b * POOL, POOL), POOL)
         v = nn(hot[rows, :], mixed[...]) + shift_row
         square = v * v
@@ -247,6 +241,36 @@
         half = 0.5 + 0.5 * t
         pool[pl.ds(b, 1), :] = jnp.sum(v * half, axis=0, keepdims=True) * (1.0 / POOL)
         slope[rows, :] = (half + 0.5 * v * (1.0 - t * t) * (root + 3.0 * cube * square)) * (1.0 / POOL)
+
+    encode(POOL, patches - 2 * POOL)
+    pl.loop(1, bins - 1)(forward)
+
+    @pl.when(me > 0)
+    def _():
+        to_left.wait_send()
+        to_right.wait_recv()
+        seen[pl.ds(0, PAD), :] = expand(halo_tok[0, PAD - 1 : PAD, :])
+
+    @pl.when(me == 0)
+    def _():
+        seen[pl.ds(0, PAD), :] = jnp.full((PAD, LANES), -1.0, F32)
+
+    @pl.when(me < last)
+    def _():
+        to_right.wait_send()
+        to_left.wait_recv()
+        seen[pl.ds(PAD + patches, PAD), :] = expand(halo_tok[1, 0:1, :])
+
+    @pl.when(me == last)
+    def _():
+        seen[pl.ds(PAD + patches, PAD), :] = jnp.full((PAD, LANES), -1.0, F32)
+
+    encode(0, POOL)
+    encode(patches - POOL, POOL)
+
+    @pl.loop(0, 2)
+    def _(side):
+        forward(side * (bins - 1))
 
     for load in (load_up, load_gain, load_pair):
         load.wait()
@@ -278,14 +302,7 @@
     def _():
         got_right[slot] = lr[...]
 
-    load_outw.wait()
-    load_cot.wait()
-    step_rows = 2 * LANES
-
-    @pl.loop(0, rows_n * cols_n // step_rows)
-    def _(i):
-        rows = pl.ds(pl.multiple_of(i * step_rows, step_rows), step_rows)
-        grid[rows, :] = nt(cot[rows, :], outw[...])
+    marks[...] = halves(joined(nt(stem_marks, hot[...])))
 
     for step in range(1, col_n):
         peer = lax.rem(col + step, col_n)
@@ -340,12 +357,6 @@
 
     sum_left[col] = part_left[pl.ds(pl.multiple_of(col * bins, bins), bins), :]
 
-    load_buck.wait()
-    member = (buck[...][None, :] == iota((BUCKETS, kernel * channels), 0)).astype(BF16)
-    stems = [nt(member[:, k * channels : (k + 1) * channels], stem[...]) for k in range(kernel)]
-    stems.append(jnp.zeros((BUCKETS, width), F32))
-    marks[...] = halves(joined(nt(halves(jnp.concatenate(stems, axis=1)), hot[...])))
-
     for step in range(1, col_n):
         peer = lax.rem(col + step, col_n)
         remote(lr, sum_left.at[peer], gl_send.at[step], gl_recv.at[peer], at(seq, peer, bat)).wait_recv()
@@ -391,18 +402,18 @@
         def _():
             copy.wait_send()
 
-    total = jnp.zeros((2 * BUCKETS, channels), F32)
     for b in range(bins):
         first = b * POOL
         cells = slope[first : first + POOL, :] * pool[b : b + 1, :]
         low = PAD if b == 0 else 0
         high = POOL - PAD if b == bins - 1 else POOL
         dpad[pl.ds(PAD + first + low, high - low), :] = cells[low:high]
-        total = total + nn(marks[:, first : first + POOL], cells.astype(BF16))
+    sums = joined(nn(marks[...], dpad[pl.ds(PAD, patches), :].astype(BF16)))
     load_proj.wait()
-    sk[...] = lax.dot_general(
-        joined(total), proj[...], (((1,), (0,)), ((), ())), precision=lax.Precision.HIGHEST, preferred_element_type=F32
-    )
+    proj_high = proj[...].astype(BF16)
+    proj_low = (proj[...] - proj_high.astype(F32)).astype(BF16)
+    sk[...] = joined(nn(halves(sums), proj_high)) + nn(sums.astype(BF16), proj_low)
+
     share = BUCKETS // col_n
 
     sends_a = []

time: 38.8 us -> 38.2 us (0.985)
  Pallas kernels: 34.7 us -> 34.2 us
    pallas_call x1, Pallas kernels: 34.7 us -> 34.2 us  [shards(): pl.pallas_call(functools.partial(body, (seq_n, col_n, batch_n)), out_shap...]
where the time goes in v3:
time: 38.2 us; the launch traced here: 38.1 us
  Pallas kernels  34.2 us (90%)
  local copies, waits for them, and re-layouts  3.27 us (9%)
  between operations  0.65 us (2%)
    pallas_call x1, Pallas kernels, shards(): pl.pallas_call(functools.partial(body, (seq_n, col_n, batch_n)), out_shap...  34.2 us
    unnamed x4, local copies, waits for them, and re-layouts  3.27 us

profile of v3, /device:TPU:0, one launch (start us, length us, event | category | flops | bytes accessed | tf_op | source)
XLA Modules:
  0.0 38.1 jit_solution(14124782697583856594)
XLA Ops:
  0.6 34.2 %shard_map.122 = (bf16[1024,768]{1,0:T(8,128)(2,1)}, f32[32,128]{1,0:T(8,128)}) custom-call(s32[128,128]{1,0:T(8,128)} %bitcast.8, bf16[64,768]{1,0:T(8,128)(2,1)} %stem_h.1, f32[768]{0:T(1024)} %bias_h.1, f32[1536]{0:T(1024)} %gain_h.1, bf16[64,1536]{1,0:T(8,128)(2,1)} %bitcast.7, f32[768,128]{1,0:T(8,128)} %proj_h.1, s32[3840]{0:T(1024)} %buck_h.1, ...), custom_call_target="tpu_custom_call" | custom-call | tf_op jit(solution)/shard_map/pallas_call | solution.py:588
  34.8 0.0 copy-start
  34.8 2.7 %copy.15 = bf16[1,1024,768]{2,1,0:T(8,128)(2,1)} copy(bf16[1,1024,768]{2,1,0:T(8,128)(2,1)} %bitcast.5) | data formatting | bytes 3145728
  37.5 0.0 copy-done
  37.5 0.6 %copy.16 = f32[1,32,128]{2,1,0:T(8,128)} copy(f32[1,32,128]{2,1,0:T(8,128)S(1)} %bitcast.9) | data formatting | bytes 32768
Async XLA Ops:
  34.8 2.7 %copy-start = (f32[32,128]{1,0:T(8,128)S(1)}, f32[32,128]{1,0:T(8,128)}, u32[]{:S(2)}) copy-start(f32[32,128]{1,0:T(8,128)} %get-tuple-element.5) | copy-start | bytes 49156
